TPU v7x, 256 devices: a whole 4x4x8 slice. The times are simulated.
256 devices in a mesh: section: 32 (over y_hi, z, core), tp: 8 (over x, y_lo).
Axes of the slice: x: 4, y: 4 (y_hi: 2, y_lo: 2; y = y_hi * 2 + y_lo), z: 8, core: 2. Of those that a mesh axis runs over, the one named last changes fastest.
Arguments:
- acts_in: bfloat16 [2, 32, 128, 6144], P(None, 'section', None, 'tp'), may hold values from -6 to 6
- cots_in: bfloat16 [2, 32, 128, 6144], P(None, 'section', None, 'tp'), may hold values from -8 to 8
- stash: bfloat16 [2, 2, 32, 128, 6144], P(None, None, 'section', None, 'tp'), may hold values from -8 to 8
- fresh_acts: bfloat16 [2, 1, 128, 6144], P(None, None, None, 'tp'), may hold values from -6 to 6
- fresh_cots: bfloat16 [2, 1, 128, 6144], P(None, None, None, 'tp'), may hold values from -8 to 8
- gains: bfloat16 [32, 6144], P('section'), may hold values from 0.5 to 1.5
- weights: bfloat16 [32, 6144, 6144], P('section', None, 'tp'), may hold values from -1.5 to 2
- adapter_a: bfloat16 [32, 8, 6144], P('section'), may hold values from -0.078125 to 0.078125
- adapter_b: bfloat16 [32, 8, 6144], P('section', None, 'tp'), may hold values from -2 to 2
Outputs:
- acts_out: bfloat16 [2, 2, 32, 128, 6144], P(None, None, 'section', None, 'tp')
- input_grads: bfloat16 [2, 2, 32, 128, 6144], P(None, None, 'section', None, 'tp')
- grad_a: bfloat16 [32, 8, 6144], P('section')
- grad_b: bfloat16 [32, 8, 6144], P('section', None, 'tp')
All inputs are finite; a program needn't handle non-finite values.
Results may differ from a plain program's by a relative error of at most 0.019.
Values may be sent and summed in bfloat16 or wider, within the bound.
A program may use at most 128 MiB of HBM per device.

v0:
```python
import jax
import jax.numpy as jnp
from jax import lax
from jax.sharding import PartitionSpec as P

EPS = 1e-05


def partner(value, axis, distance):
    mask = 2**distance
    pairs = [(source, source ^ mask) for source in range(lax.axis_size(axis))]
    return lax.ppermute(value, axis, pairs)


def from_behind(value, axis, steps):
    count = lax.axis_size(axis)
    initial, last = (max(0, -steps), min(count, count - steps))
    return lax.ppermute(value, axis, [(source, source + steps) for source in range(initial, last)])


def normalize(floats, gain):
    inv_rms = lax.rsqrt(jnp.mean(floats * floats, axis=-1, keepdims=True) + EPS)
    unit = floats * inv_rms
    normed = (unit * gain.astype(jnp.float32)).astype(jnp.bfloat16)
    return (inv_rms, unit, normed)


def reverse_section(values):
    steps = lax.axis_size("section").bit_length() - 1
    for which in range(steps):
        values = partner(values, "section", which)
    return values


def pass_on(values, amount):
    return from_behind(values, "section", amount)


def contract_last(left, right):
    return lax.dot_general(
        left, right, (((1,), (1,)), ((), ())), preferred_element_type=jnp.float32
    )


def contract_first(left, right):
    return lax.dot_general(
        left, right, (((0,), (0,)), ((), ())), preferred_element_type=jnp.float32
    )


def forward_block(full_rows, own, gain, weight, lower, upper):
    pairs, micro, width = full_rows.shape
    columns = own.shape[2]
    total_rows = pairs * micro
    floats = full_rows.astype(jnp.float32).reshape(total_rows, width)
    inv_rms, unit, normed = normalize(floats, gain)
    latent = contract_last(normed, lower).astype(jnp.bfloat16)
    result = own.astype(jnp.float32).reshape(total_rows, columns)
    result = result + jnp.dot(normed, weight, preferred_element_type=jnp.float32)
    result = result + jnp.dot(latent, upper, preferred_element_type=jnp.float32)
    return result.astype(jnp.bfloat16).reshape(pairs, micro, columns)


def backward_block(full_rows, cotangent, gain, weight, lower, upper, offset):
    pairs, micro, width = full_rows.shape
    columns = cotangent.shape[2]
    total_rows = pairs * micro
    floats = full_rows.astype(jnp.float32).reshape(total_rows, width)
    inv_rms, unit, normed = normalize(floats, gain)
    latent = contract_last(normed, lower).astype(jnp.bfloat16)
    flat = cotangent.reshape(total_rows, columns)
    gain_f = gain.astype(jnp.float32)
    lower_f = lower.astype(jnp.float32)
    low_part = lax.optimization_barrier(contract_last(flat, upper).astype(jnp.bfloat16)).astype(
        jnp.float32
    )
    base_part = contract_last(flat, weight)
    base, low_sum = (
        lax.psum(base_part.astype(jnp.bfloat16), "tp").astype(jnp.float32),
        lax.psum(low_part.astype(jnp.bfloat16), "tp").astype(jnp.float32),
    )
    grad_norm = base + jnp.dot(low_sum, lower_f, precision=lax.Precision.HIGHEST)
    stat = jnp.mean(gain_f * unit * grad_norm, axis=-1, keepdims=True)
    full_back = inv_rms * (gain_f * grad_norm - unit * stat)
    back = flat.astype(jnp.float32) + lax.dynamic_slice_in_dim(full_back, offset, columns, 1)
    grad_lower = contract_first(low_sum.astype(jnp.bfloat16), normed)
    grad_upper = contract_first(latent, flat)
    return (back.astype(jnp.bfloat16).reshape(pairs, micro, columns), grad_lower, grad_upper)


def body(acts_in, cots_in, stash, fresh_acts, fresh_cots, gains, weights, adapter_a, adapter_b):
    ticks = stash.shape[1]
    columns = acts_in.shape[3]
    gain = gains[0]
    weight = weights[0]
    lower = adapter_a[0]
    upper = adapter_b[0]
    offset = lax.axis_index("tp") * columns
    position = lax.axis_index("section")
    last_section = lax.axis_size("section") - 1
    upward = jnp.concatenate([acts_in[1, 0][None], cots_in[1, 0][None], stash[1, :, 0]], axis=0)
    moved = reverse_section(upward)
    current = jnp.stack([acts_in[0, 0], moved[0]])
    cotangent = jnp.stack([cots_in[0, 0], moved[1]])
    kept = jnp.stack([stash[0, :, 0], moved[2:]])
    grad_lower = jnp.zeros(lower.shape, jnp.float32)
    grad_upper = jnp.zeros(upper.shape, jnp.float32)
    outputs = []
    backs = []
    for tick in range(ticks):
        full_rows = lax.all_gather(
            jnp.concatenate([current, kept[:, tick]], axis=0), "tp", axis=2, tiled=True
        )
        ahead = forward_block(full_rows[:2], current, gain, weight, lower, upper)
        back, lower_term, upper_term = backward_block(
            full_rows[2:], cotangent, gain, weight, lower, upper, offset
        )
        grad_lower = grad_lower + lower_term
        grad_upper = grad_upper + upper_term
        outputs.append(ahead)
        backs.append(back)
        if tick + 1 < ticks:
            current = jnp.where(position == 0, fresh_acts[:, tick], pass_on(ahead, 1))
            cotangent = jnp.where(position == last_section, fresh_cots[:, tick], pass_on(back, -1))
    ahead_all = jnp.stack(outputs)
    back_all = jnp.stack(backs)
    returned = reverse_section(jnp.concatenate([ahead_all[:, 1], back_all[:, 1]], axis=0))
    acts_out = jnp.stack([ahead_all[:, 0], returned[:ticks]])[:, :, None]
    input_grads = jnp.stack([back_all[:, 0], returned[ticks:]])[:, :, None]
    return (
        acts_out,
        input_grads,
        grad_lower.astype(jnp.bfloat16)[None],
        grad_upper.astype(jnp.bfloat16)[None],
    )


def solution(mesh):
    in_specs = (
        P(None, "section", None, "tp"),
        P(None, "section", None, "tp"),
        P(None, None, "section", None, "tp"),
        P(None, None, None, "tp"),
        P(None, None, None, "tp"),
        P("section", None),
        P("section", None, "tp"),
        P("section", None, None),
        P("section", None, "tp"),
    )
    out_specs = (
        P(None, None, "section", None, "tp"),
        P(None, None, "section", None, "tp"),
        P("section", None, None),
        P("section", None, "tp"),
    )
    return jax.shard_map(body, mesh=mesh, in_specs=in_specs, out_specs=out_specs, check_vma=False)
```

profile of v0, /device:TPU:8, one launch (start us, length us, event | category | flops | bytes accessed | tf_op | source)
XLA Modules:
  0.0 838.5 jit_solution(1836829401466387121)
XLA Ops:
  7.2 1.2 slice_bitcast_fusion.3
  8.4 1.3 slice_bitcast_fusion.5
  9.9 2.3 collective-permute-done
  12.1 1.9 collective-permute-start.1
  14.1 17.8 %collective-permute-done.1 = bf16[4,128,768]{2,1,0:T(8,128)(2,1)S(1)} collective-permute-done((bf16[4,128,768]{2,1,0:T(8,128)(2,1)S(1)}, bf16[4,128,768]{2,1,0:T(8,128)(2,1)S(1)}, u32[]{:S(2)}, u32[]{:S(2)}) %collective-permute-start.1) | collective-permute-done | bytes 786464 | tf_op jit(solution)/shard_map/ppermute | solution.py:12
  31.9 3.3 collective-permute-start.2
  35.2 34.1 %collective-permute-done.2 = bf16[4,128,768]{2,1,0:T(8,128)(2,1)S(1)} collective-permute-done((bf16[4,128,768]{2,1,0:T(8,128)(2,1)S(1)}, bf16[4,128,768]{2,1,0:T(8,128)(2,1)S(1)}, u32[]{:S(2)}, u32[]{:S(2)}) %collective-permute-start.2) | collective-permute-done | bytes 786464 | tf_op jit(solution)/shard_map/ppermute | solution.py:12
  69.2 6.2 collective-permute-start.3
  75.4 34.4 %collective-permute-done.3 = bf16[4,128,768]{2,1,0:T(8,128)(2,1)S(1)} collective-permute-done((bf16[4,128,768]{2,1,0:T(8,128)(2,1)S(1)}, bf16[4,128,768]{2,1,0:T(8,128)(2,1)S(1)}, u32[]{:S(2)}, u32[]{:S(2)}) %collective-permute-start.3) | collective-permute-done | bytes 786464 | tf_op jit(solution)/shard_map/ppermute | solution.py:12
  109.8 2.3 collective-permute-start.4
  112.1 17.5 %collective-permute-done.4 = bf16[4,128,768]{2,1,0:T(8,128)(2,1)S(1)} collective-permute-done((bf16[4,128,768]{2,1,0:T(8,128)(2,1)S(1)}, bf16[4,128,768]{2,1,0:T(8,128)(2,1)S(1)}, u32[]{:S(2)}, u32[]{:S(2)}) %collective-permute-start.4) | collective-permute-done | bytes 786464 | tf_op jit(solution)/shard_map/ppermute | solution.py:12
  129.6 0.8 fusion.50
  130.5 1.0 pad_maximum_fusion.1
  131.6 0.8 pad_maximum_fusion.7
  132.4 0.7 copy-done.5
  133.1 11.1 %fusion.8 = bf16[256,6144]{1,0:T(8,128)(2,1)} fusion(bf16[256,768]{1,0:T(8,128)(2,1)S(1)} %bitcast.149, bf16[1,6144,768]{2,1,0:T(8,128)(2,1)} %param.15), kind=kOutput, calls=%fused_computation.14 | convolution fusion | flops 2417491968 | bytes 12976128 | tf_op jit(solution)/shard_map/dot_general | solution.py:40
  144.3 117.1 %all-gather.3.cloned.1.call-done = bf16[4,128,6144]{2,1,0:T(8,128)(2,1)} async-done(((bf16[4,128,768]{2,1,0:T(8,128)(2,1)}), bf16[4,128,6144]{2,1,0:T(8,128)(2,1)}) %all-gather.3.cloned.1.call-update) | async-done | bytes 6291472 | tf_op jit(solution)/shard_map/all_gather | solution.py:111
  261.4 3.7 fusion.16
  265.2 0.9 copy-done.1
  266.1 3.0 multiply_convert_fusion.1
  269.1 1.8 copy-done.18
  270.9 3.5 fusion.6
  274.4 3.3 fusion.25
  277.7 1.3 collective-permute-start.5
  279.0 1.5 collective-permute-done.5
  280.5 1.0 bitcast_select_fusion.1
  281.6 0.7 copy-done.10
  282.3 1.9 pad_maximum_fusion.2
  284.4 1.2 convolution_convert_fusion.5
  285.6 20.4 %psum.29 = bf16[256,8]{0,1:T(8,128)(2,1)S(1)} all-reduce(bf16[256,8]{0,1:T(8,128)(2,1)S(1)} %convolution_convert_fusion.5), channel_id=1, replica_groups=mesh['section'=32,'tp'=8] {'tp'}, use_global_device_ids=true, to_apply=%region_4.0 | all-reduce | flops 2048 | bytes 8192 | tf_op jit(solution)/shard_map/psum | solution.py:80
  306.1 5.3 slice_convert_fusion.1
  311.3 103.1 %all-reduce.3.cloned.1.call-done = bf16[256,6144]{1,0:T(8,128)(2,1)} async-done(((bf16[256,6144]{1,0:T(8,128)(2,1)}), bf16[256,6144]{1,0:T(8,128)(2,1)}) %all-reduce.3.cloned.1.call-update) | async-done | bytes 3145744 | tf_op jit(solution)/shard_map/psum | solution.py:79
  414.5 5.5 multiply_reduce_fusion.2
  420.0 2.6 copy-done.3
  422.6 0.2 fusion.39
  422.8 1.3 collective-permute-start.6
  424.2 2.3 collective-permute-done.6
  426.7 23.4 %psum.31 = bf16[256,8]{0,1:T(8,128)(2,1)S(1)} all-reduce(bf16[256,8]{0,1:T(8,128)(2,1)S(1)} %convolution_convert_fusion.4), channel_id=1, replica_groups=mesh['section'=32,'tp'=8] {'tp'}, use_global_device_ids=true, to_apply=%region_8.9 | all-reduce | flops 2048 | bytes 8192 | tf_op jit(solution)/shard_map/psum | solution.py:80
  450.1 11.2 %fusion.11 = bf16[256,6144]{1,0:T(8,128)(2,1)} fusion(bf16[256,768]{1,0:T(8,128)(2,1)S(1)} %bitcast.153, bf16[1,6144,768]{2,1,0:T(8,128)(2,1)} %param.15), kind=kOutput, calls=%fused_computation.15 | convolution fusion | flops 2417491968 | bytes 12976128 | tf_op jit(solution)/shard_map/dot_general | solution.py:40
  461.3 88.1 %all-gather.5.cloned.1.call-done = bf16[4,128,6144]{2,1,0:T(8,128)(2,1)} async-done(((bf16[4,128,768]{2,1,0:T(8,128)(2,1)}), bf16[4,128,6144]{2,1,0:T(8,128)(2,1)}) %all-gather.5.cloned.1.call-update) | async-done | bytes 6291472 | tf_op jit(solution)/shard_map/all_gather | solution.py:111
  549.4 3.7 fusion.19
  553.1 0.9 copy-done.2
  554.0 3.1 multiply_convert_fusion
  557.1 7.1 fusion.4
  564.3 3.3 fusion.41
  567.5 5.5 slice_convert_fusion
  573.1 131.2 %all-reduce.5.cloned.1.call-done = bf16[256,6144]{1,0:T(8,128)(2,1)} async-done(((bf16[256,6144]{1,0:T(8,128)(2,1)}), bf16[256,6144]{1,0:T(8,128)(2,1)}) %all-reduce.5.cloned.1.call-update) | async-done | bytes 3145744 | tf_op jit(solution)/shard_map/psum | solution.py:79
  704.3 5.6 multiply_reduce_fusion
  710.4 0.3 collective-permute-start.7
  710.7 2.3 collective-permute-done.7
  713.0 1.6 collective-permute-start.8
  714.5 18.0 %collective-permute-done.8 = bf16[4,128,768]{2,1,0:T(8,128)(2,1)S(1)} collective-permute-done((bf16[4,128,768]{2,1,0:T(8,128)(2,1)S(1)}, bf16[4,128,768]{2,1,0:T(8,128)(2,1)S(1)}, u32[]{:S(2)}, u32[]{:S(2)}) %collective-permute-start.8) | collective-permute-done | bytes 786464 | tf_op jit(solution)/shard_map/ppermute | solution.py:12
  732.6 2.5 collective-permute-start.9
  735.1 34.0 %collective-permute-done.9 = bf16[4,128,768]{2,1,0:T(8,128)(2,1)S(1)} collective-permute-done((bf16[4,128,768]{2,1,0:T(8,128)(2,1)S(1)}, bf16[4,128,768]{2,1,0:T(8,128)(2,1)S(1)}, u32[]{:S(2)}, u32[]{:S(2)}) %collective-permute-start.9) | collective-permute-done | bytes 786464 | tf_op jit(solution)/shard_map/ppermute | solution.py:12
  769.1 5.7 collective-permute-start.10
  774.8 0.5 fusion.22
  775.3 34.4 %collective-permute-done.10 = bf16[4,128,768]{2,1,0:T(8,128)(2,1)} collective-permute-done((bf16[4,128,768]{2,1,0:T(8,128)(2,1)S(1)}, bf16[4,128,768]{2,1,0:T(8,128)(2,1)}, u32[]{:S(2)}, u32[]{:S(2)}) %collective-permute-start.10) | collective-permute-done | bytes 786464 | tf_op jit(solution)/shard_map/ppermute | solution.py:12
  809.7 2.1 collective-permute-start.11
  811.8 3.0 fusion.27
  814.9 3.7 fusion.31
  818.5 3.9 fusion.15
  822.5 7.5 collective-permute-done.11
  830.1 0.9 maximum_bitcast_fusion.1
  831.0 0.9 maximum_bitcast_fusion
  (65 shorter events, 1.4 us)
Async XLA Ops:
  7.2 267.2 %copy-start = (bf16[1,8,6144]{2,1,0:T(8,128)(2,1)S(1)}, bf16[1,8,6144]{2,1,0:T(8,128)(2,1)}, u32[]{:S(2)}) copy-start(bf16[1,8,6144]{2,1,0:T(8,128)(2,1)} %param.16) | copy-start | bytes 294916
  7.2 124.3 %copy-start.17 = (bf16[1,6144]{1,0:T(2,128)(2,1)S(1)}, bf16[1,6144]{1,0:T(2,128)(2,1)}, u32[]{:S(2)}) copy-start(bf16[1,6144]{1,0:T(2,128)(2,1)} %param.14) | copy-start | bytes 36868
  7.2 254.3 %all-gather.3.cloned.1.call-start = ((), (), s32[]{:S(2)}) async-start(), calls=%async_computation | async-start | bytes 7077888 | tf_op jit(solution)/shard_map/all_gather | solution.py:111
  9.8 2.4 collective-permute-start
  12.1 19.8 %collective-permute-start.1 = (bf16[4,128,768]{2,1,0:T(8,128)(2,1)S(1)}, bf16[4,128,768]{2,1,0:T(8,128)(2,1)S(1)}, u32[]{:S(2)}, u32[]{:S(2)}) collective-permute-start(bf16[4,128,768]{2,1,0:T(8,128)(2,1)S(1)} %collective-permute-done), channel_id=1, source_target_pairs={{0,16},{8,24},{16,0},{24,8},{32,48},{40,56},{48,32},{56,40},{64,80... | collective-permute-start | bytes 2359304 | tf_op jit(solution)/shard_map/ppermute | solution.py:12
  31.9 37.3 %collective-permute-start.2 = (bf16[4,128,768]{2,1,0:T(8,128)(2,1)S(1)}, bf16[4,128,768]{2,1,0:T(8,128)(2,1)S(1)}, u32[]{:S(2)}, u32[]{:S(2)}) collective-permute-start(bf16[4,128,768]{2,1,0:T(8,128)(2,1)S(1)} %collective-permute-done.1), channel_id=1, source_target_pairs={{0,32},{8,40},{16,48},{24,56},{32,0},{40,8},{48,16},{56,24},{64,96... | collective-permute-start | bytes 2359304 | tf_op jit(solution)/shard_map/ppermute | solution.py:12
  69.2 40.6 %collective-permute-start.3 = (bf16[4,128,768]{2,1,0:T(8,128)(2,1)S(1)}, bf16[4,128,768]{2,1,0:T(8,128)(2,1)S(1)}, u32[]{:S(2)}, u32[]{:S(2)}) collective-permute-start(bf16[4,128,768]{2,1,0:T(8,128)(2,1)S(1)} %collective-permute-done.2), channel_id=1, source_target_pairs={{0,64},{8,72},{16,80},{24,88},{32,96},{40,104},{48,112},{56,120},{... | collective-permute-start | bytes 2359304 | tf_op jit(solution)/shard_map/ppermute | solution.py:12
  109.8 19.8 %collective-permute-start.4 = (bf16[4,128,768]{2,1,0:T(8,128)(2,1)S(1)}, bf16[4,128,768]{2,1,0:T(8,128)(2,1)S(1)}, u32[]{:S(2)}, u32[]{:S(2)}) collective-permute-start(bf16[4,128,768]{2,1,0:T(8,128)(2,1)S(1)} %collective-permute-done.3), channel_id=1, source_target_pairs={{0,128},{8,136},{16,144},{24,152},{32,160},{40,168},{48,176},{56,1... | collective-permute-start | bytes 2359304 | tf_op jit(solution)/shard_map/ppermute | solution.py:12
  131.5 283.0 %all-reduce.3.cloned.1.call-start = ((), (), s32[]{:S(2)}) async-start(), calls=%async_computation.2 | async-start | bytes 6291456 | tf_op jit(solution)/shard_map/psum | solution.py:79
  132.4 0.8 copy-start.5
  144.2 405.1 %all-gather.5.cloned.1.call-start = ((), (), s32[]{:S(2)}) async-start(), calls=%async_computation.1 | async-start | bytes 7077888 | tf_op jit(solution)/shard_map/all_gather | solution.py:111
  261.4 4.7 copy-start.1
  266.1 4.8 copy-start.18
  270.9 3.5 copy-start.16
  277.7 2.8 collective-permute-start.5
  281.6 0.7 copy-start.10
  284.3 419.9 %all-reduce.5.cloned.1.call-start = ((), (), s32[]{:S(2)}) async-start(), calls=%async_computation.3 | async-start | bytes 6291456 | tf_op jit(solution)/shard_map/psum | solution.py:79
  414.5 8.1 copy-start.6
  414.5 12.0 %copy-start.15 = (bf16[2,1,128,768]{3,2,1,0:T(8,128)(2,1)S(1)}, bf16[2,1,128,768]{3,2,1,0:T(8,128)(2,1)}, u32[]{:S(2)}) copy-start(bf16[2,1,128,768]{3,2,1,0:T(8,128)(2,1)} %param.13) | copy-start | bytes 1179652
  419.9 2.6 copy-start.3
  422.8 1.3 copy-start.11
  422.8 3.6 collective-permute-start.6
  426.5 34.8 %copy-start.8 = (bf16[2,128,768]{2,1,0:T(8,128)(2,1)}, bf16[2,128,768]{2,1,0:T(8,128)(2,1)S(1)}, u32[]{:S(2)}) copy-start(bf16[2,128,768]{2,1,0:T(8,128)(2,1)S(1)} %bitcast_select_fusion) | copy-start | bytes 1179652
  549.4 4.7 copy-start.2
  704.2 70.6 %slice-start = ((s8[6291456]{0:T(1024)(128)(4,1)}), s8[4194304]{0:T(1024)(128)(4,1)S(1)}, s32[]{:S(2)}) async-start(s8[6291456]{0:T(1024)(128)(4,1)} %bitcast.143), calls=%async_computation.4 | async-start | bytes 8388608
  704.2 5.6 copy-start.13
  704.2 5.6 copy-start.14
  704.2 5.7 copy-start.9
  704.2 6.0 copy-start.12
  704.2 70.6 %slice-start.1 = ((s8[6291456]{0:T(1024)(128)(4,1)}), s8[2097152]{0:T(1024)(128)(4,1)S(1)}, s32[]{:S(2)}) async-start(s8[6291456]{0:T(1024)(128)(4,1)} %bitcast.143), calls=%async_computation.5 | async-start | bytes 4194304
  709.8 65.5 %copy-start.4 = (f32[256,6144]{1,0:T(8,128)}, f32[256,6144]{1,0:T(8,128)S(1)}, u32[]{:S(2)}) copy-start(f32[256,6144]{1,0:T(8,128)S(1)} %get-tuple-element.9) | copy-start | bytes 18874372
  710.3 104.6 %copy-start.7 = (bf16[2,128,768]{2,1,0:T(8,128)(2,1)S(1)}, bf16[2,128,768]{2,1,0:T(8,128)(2,1)}, u32[]{:S(2)}) copy-start(bf16[2,128,768]{2,1,0:T(8,128)(2,1)} %copy-done.5) | copy-start | bytes 1179652
  710.4 2.6 collective-permute-start.7
  713.0 19.6 %collective-permute-start.8 = (bf16[4,128,768]{2,1,0:T(8,128)(2,1)S(1)}, bf16[4,128,768]{2,1,0:T(8,128)(2,1)S(1)}, u32[]{:S(2)}, u32[]{:S(2)}) collective-permute-start(bf16[4,128,768]{2,1,0:T(8,128)(2,1)S(1)} %collective-permute-done.7), channel_id=1, source_target_pairs={{0,16},{8,24},{16,0},{24,8},{32,48},{40,56},{48,32},{56,40},{64,80... | collective-permute-start | bytes 2359304 | tf_op jit(solution)/shard_map/ppermute | solution.py:12
  732.6 36.5 %collective-permute-start.9 = (bf16[4,128,768]{2,1,0:T(8,128)(2,1)S(1)}, bf16[4,128,768]{2,1,0:T(8,128)(2,1)S(1)}, u32[]{:S(2)}, u32[]{:S(2)}) collective-permute-start(bf16[4,128,768]{2,1,0:T(8,128)(2,1)S(1)} %collective-permute-done.8), channel_id=1, source_target_pairs={{0,32},{8,40},{16,48},{24,56},{32,0},{40,8},{48,16},{56,24},{64,96... | collective-permute-start | bytes 2359304 | tf_op jit(solution)/shard_map/ppermute | solution.py:12
  769.1 40.7 %collective-permute-start.10 = (bf16[4,128,768]{2,1,0:T(8,128)(2,1)S(1)}, bf16[4,128,768]{2,1,0:T(8,128)(2,1)}, u32[]{:S(2)}, u32[]{:S(2)}) collective-permute-start(bf16[4,128,768]{2,1,0:T(8,128)(2,1)S(1)} %collective-permute-done.9), channel_id=1, source_target_pairs={{0,64},{8,72},{16,80},{24,88},{32,96},{40,104},{48,112},{56,120},{... | collective-permute-start | bytes 2359304 | tf_op jit(solution)/shard_map/ppermute | solution.py:12
  809.7 20.3 %collective-permute-start.11 = (bf16[4,128,768]{2,1,0:T(8,128)(2,1)}, bf16[4,128,768]{2,1,0:T(8,128)(2,1)S(1)}, u32[]{:S(2)}, u32[]{:S(2)}) collective-permute-start(bf16[4,128,768]{2,1,0:T(8,128)(2,1)} %collective-permute-done.10), channel_id=1, source_target_pairs={{0,128},{8,136},{16,144},{24,152},{32,160},{40,168},{48,176},{56,1... | collective-permute-start | bytes 2359304 | tf_op jit(solution)/shard_map/ppermute | solution.py:12
Sparse Core Ops, SparseCore 0:
  131.6 129.8 all-gather.2
  264.1 150.2 all-reduce.2
  416.8 132.5 all-gather.4
  551.9 152.2 all-reduce.4
where the time goes:
time: 840 us; the launch traced here: 838 us
  waiting for transfers between devices  646 us (77%)
  matrix products  63 us (8%)
  blocking collectives  43.9 us (5%)
  other arithmetic  32.6 us (4%)
  starting transfers between devices  28.8 us (3%)
  between operations  14.1 us (2%)
  local copies, waits for them, and re-layouts  10.5 us (1%)
    psum x2, waiting for transfers between devices, backward_block(): lax.psum(base_part.astype(jnp.bfloat16), 'tp').astype(jnp.float32)  234 us
    all_gather x2, waiting for transfers between devices, body(): lax.all_gather(jnp.concatenate([current, kept[:, tick]], axis=0), 'tp', a...  205 us
    ppermute x10, waiting for transfers between devices, partner(): return lax.ppermute(value, axis, pairs)  202 us
    psum x2, blocking collectives, backward_block(): lax.psum(low_part.astype(jnp.bfloat16), 'tp').astype(jnp.float32)  43.9 us
    ppermute x10, starting transfers between devices, partner(): return lax.ppermute(value, axis, pairs)  26 us
    dot_general x4, matrix products, contract_last(): lax.dot_general(left, right, (((1,), (1,)), ((), ())), preferred_element_...  23.6 us
  transfers between devices with their start and end apart: 16, of which 16 were waited for; matrix products, arithmetic and copies ran while one was open for 10% of the time, Pallas kernels for 0%

commit v1 on v0

v1 whole, which is shorter than its diff:
```python
import jax
import jax.numpy as jnp
from jax import lax
from jax.experimental import pallas as pl
from jax.experimental.pallas import tpu as pltpu
from jax.sharding import PartitionSpec as P

EPS = 1e-05
MESH = pl.DeviceIdType.MESH
F32 = jnp.float32
BF16 = jnp.bfloat16

D0, U0, D1, U1 = range(4)


def contract_last(left, right):
    return lax.dot_general(left, right, (((1,), (1,)), ((), ())), preferred_element_type=F32)


def contract_first(left, right):
    return lax.dot_general(left, right, (((0,), (0,)), ((), ())), preferred_element_type=F32)


def kernel(
    acts, cots, stash, fresh_acts, fresh_cots, gain, weights, lower, upper,
    acts_out, grads_out, grad_a, grad_b,
    w, x, c, s, fa, fc, ps, pr, yb, gb, sm, gar, acc, acc_g, sq, left, right, ga_acc, gb_acc,
    w_sem, in_sem, out_sem,
    ag_s, ag_r, rs_s, rs_r, sm_s, sm_r, sh_s, sh_r, ri_s, ri_r, ro_s, ro_r, ga_s, ga_r,
):
    sec, tp = lax.axis_index("section"), lax.axis_index("tp")
    n_sec, n_tp = lax.axis_size("section"), lax.axis_size("tp")
    cols = w.shape[1]
    width = n_tp * cols
    rank = lower.shape[1]
    nx = n_tp // 2
    xi, yi = tp // 2, tp % 2
    turn = 1 - 2 * yi
    xp, xm, x2 = (xi + turn + nx) % nx, (xi - turn + nx) % nx, (xi + 2) % nx
    yo = 1 - yi
    own, across = tp, xi * 2 + yo
    pp, po, mm, mo, tt, to = xp * 2 + yi, xp * 2 + yo, xm * 2 + yi, xm * 2 + yo, x2 * 2 + yi, x2 * 2 + yo
    ahead, behind, mirror = (sec + 1) % n_sec, (sec + n_sec - 1) % n_sec, n_sec - 1 - sec
    sends = []

    def send(src, dst, send_sem, recv_sem, to_sec, to_tp):
        copy = pltpu.make_async_remote_copy(
            src_ref=src, dst_ref=dst, send_sem=send_sem, recv_sem=recv_sem,
            device_id=(to_sec, to_tp), device_id_type=MESH,
        )
        copy.start()
        sends.append(copy)
        return copy

    def block(index):
        return pl.ds(pl.multiple_of(index * cols, cols), cols)

    order = (tt, to, po, mm, pp, mo, across, own)
    loads = [
        pltpu.make_async_copy(acts.at[0, 0], x.at[D0, own], in_sem.at[0]),
        pltpu.make_async_copy(cots.at[0, 0], c.at[D0], in_sem.at[1]),
    ]
    w_loads = [
        pltpu.make_async_copy(weights.at[0, block(which)], w.at[block(which)], w_sem.at[i])
        for i, which in enumerate(order)
    ]
    loads += [
        pltpu.make_async_copy(stash.at[0, 0, 0], s.at[D0], in_sem.at[2]),
        pltpu.make_async_copy(stash.at[0, 1, 0], s.at[D1], in_sem.at[3]),
        pltpu.make_async_copy(fresh_acts.at[:, 0], fa, in_sem.at[4]),
        pltpu.make_async_copy(fresh_cots.at[:, 0], fc, in_sem.at[5]),
    ]
    for copy in loads[:2] + w_loads + loads[2:]:
        copy.start()

    barrier = pltpu.get_barrier_semaphore()
    peers = [(sec, (tp + k) % n_tp) for k in range(1, n_tp)]
    peers += [(mirror, tp), (ahead, tp), (behind, tp)]
    for peer in peers:
        pl.semaphore_signal(barrier, inc=1, device_id=peer, device_id_type=MESH)
    pl.semaphore_wait(barrier, len(peers))

    rev_c = send(cots.at[1, 0], c.at[U0], ri_s.at[0], ri_r.at[0], mirror, tp)
    rev_x = send(acts.at[1, 0], x.at[U0, own], ri_s.at[1], ri_r.at[1], mirror, tp)
    rev_s = {
        U0: send(stash.at[1, 0, 0], s.at[U0], ri_s.at[2], ri_r.at[2], mirror, tp),
        U1: send(stash.at[1, 1, 0], s.at[U1], ri_s.at[3], ri_r.at[3], mirror, tp),
    }

    left[0:rank] = lower[0].astype(F32)
    left[rank:2 * rank] = jnp.broadcast_to(gain[...].astype(F32), (rank, width))
    row = lax.broadcasted_iota(jnp.int32, (rank, 128), 0)
    right[0:rank, 0:cols] = upper[0].astype(F32)
    right[rank:2 * rank, 0:cols] = jnp.zeros((rank, cols), F32)
    right[0:rank, cols:cols + 128] = jnp.zeros((rank, 128), F32)
    right[rank:2 * rank, cols:cols + 128] = jnp.where(row == 0, 1.0, 0.0).astype(F32)
    ga_acc[...] = jnp.zeros_like(ga_acc)
    gb_acc[...] = jnp.zeros_like(gb_acc)

    def build(i):
        w_loads[i].wait()
        base = order[i] * cols

        def step(j, carry):
            at = pl.ds(pl.multiple_of(base + j * 128, 128), 128)
            both = contract_first(left[:, at].astype(BF16), right[...].astype(BF16))
            scale = both[:, cols:cols + 128]
            for k in range(cols // 128):
                lanes = slice(k * 128, (k + 1) * 128)
                w[at, lanes] = ((w[at, lanes].astype(F32) + both[:, lanes]) * scale).astype(BF16)
            return carry

        lax.fori_loop(0, cols // 128, step, 0)

    gathered = {}

    def ag0(u):
        mine = x.at[u, own]
        gathered[u] = [
            send(mine, mine, ag_s.at[u, 0], ag_r.at[u, 0], sec, across),
            send(mine, mine, ag_s.at[u, 1], ag_r.at[u, 1], sec, pp),
            send(mine, mine, ag_s.at[u, 2], ag_r.at[u, 2], sec, mm),
        ]

    def ag1(u):
        gathered[u][0].wait_recv()
        part = x.at[u, across]
        gathered[u] += [
            send(part, part, ag_s.at[u, 3], ag_r.at[u, 3], sec, pp),
            send(part, part, ag_s.at[u, 4], ag_r.at[u, 4], sec, mm),
        ]

    def ag2(u):
        gathered[u][1].wait_recv()
        part = x.at[u, mm]
        gathered[u].append(send(part, part, ag_s.at[u, 5], ag_r.at[u, 5], sec, pp))

    def ag3(u):
        gathered[u][4].wait_recv()
        part = x.at[u, po]
        gathered[u].append(send(part, part, ag_s.at[u, 6], ag_r.at[u, 6], sec, mm))

    def fwd(u, which, first=False):
        rows = x[u, which]
        floats = rows.astype(F32)
        squares = floats * floats
        total = squares[:, 0:128]
        for k in range(1, cols // 128):
            total = total + squares[:, k * 128:(k + 1) * 128]
        product = jnp.dot(rows, w[block(which), :], preferred_element_type=F32)
        if first:
            sq[u] = total
            acc[u] = product
        else:
            sq[u] += total
            acc[u] += product

    def fwd_near(u):
        fwd(u, own, True)
        fwd(u, across)
        fwd(u, mm)
        gathered[u][2].wait_recv()
        fwd(u, pp)
        gathered[u][3].wait_recv()
        fwd(u, mo)
        fwd(u, po)

    def fwd_far(u):
        gathered[u][5].wait_recv()
        fwd(u, tt)
        gathered[u][6].wait_recv()
        fwd(u, to)
        inv = lax.rsqrt(jnp.sum(sq[u], axis=1, keepdims=True) / width + EPS)
        yb[u] = (x[u, own].astype(F32) + inv * acc[u]).astype(BF16)
        finish(u, yb.at[u], acts_out, 0)

    shifted, outs, returned = {}, [], []

    def finish(u, result, out, which):
        if u < 2:
            if which == 0:
                shifted[u, 0] = send(result, x.at[u + 2, own], sh_s.at[u, 0], sh_r.at[u, 0], ahead, tp)
            else:
                shifted[u, 1] = send(result, c.at[u + 2], sh_s.at[u, 1], sh_r.at[u, 1], behind, tp)
        tick, relay = u // 2, u % 2
        if relay == 0:
            copy = pltpu.make_async_copy(result, out.at[0, tick, 0], out_sem.at[tick * 2 + which])
            copy.start()
            outs.append(copy)
        else:
            k = tick * 2 + which
            returned.append(send(result, out.at[1, tick, 0], ro_s.at[k], ro_r.at[k], mirror, tp))

    def take_x(u):
        shifted[u, 0].wait_recv()

        @pl.when(sec == 0)
        def _():
            x[u + 2, own] = fa[u]

    def take_c(u):
        shifted[u, 1].wait_recv()

        @pl.when(sec == n_sec - 1)
        def _():
            c[u + 2] = fc[u]

    reduced = {}

    def part(u, which):
        return contract_last(c[u], w[block(which), :])

    def rs_send(u, i, value, to_tp):
        ps[u, i] = value.astype(BF16)
        reduced.setdefault(u, {})[i] = send(
            ps.at[u, i], pr.at[u, i], rs_s.at[u, i], rs_r.at[u, i], sec, to_tp
        )

    def got(u, i):
        reduced[u][i].wait_recv()
        return pr[u, i].astype(F32)

    def rs0(u):
        rs_send(u, 0, part(u, tt), pp)
        rs_send(u, 1, part(u, to), mm)

    def rs1(u):
        rs_send(u, 2, part(u, po), pp)
        rs_send(u, 3, part(u, mm), mm)

    def rs2(u):
        rs_send(u, 4, part(u, pp) + got(u, 0), pp)
        rs_send(u, 5, part(u, mo) + got(u, 1), mm)

    def rs3(u):
        rs_send(u, 6, part(u, across) + got(u, 5) + got(u, 2), across)

    summed = {}

    def split_sum(value):
        ones = jnp.ones((16, cols), BF16)
        high = value.astype(BF16)
        low = (value - high.astype(F32)).astype(BF16)
        return (contract_last(ones, high) + contract_last(ones, low))[0:8]

    def rs4(u):
        total = part(u, own) + got(u, 4) + got(u, 3) + got(u, 6)
        acc_g[u] = total
        floats = s[u].astype(F32)
        at = block(own)
        pair = jnp.concatenate([left[0:rank, at] * left[rank:2 * rank, at], right[0:rank, 0:cols]], axis=0).astype(BF16)
        sm[u, own, 0:8] = contract_last(pair, c[u])[8:16]
        sm[u, own, 8:16] = contract_last(pair, s[u])[0:8]
        sm[u, own, 16:24] = split_sum(floats * floats)
        sm[u, own, 24:32] = split_sum(floats * total)
        mine = sm.at[u, own]
        summed[u] = [
            send(mine, mine, sm_s.at[u, k - 1], sm_r.at[u, k - 1], sec, (tp + k) % n_tp)
            for k in range(1, n_tp)
        ]

    def rs5(u):
        for copy in summed[u]:
            copy.wait_recv()
        total = jnp.sum(sm[u], axis=0)
        low, latent = total[0:8], total[8:16]
        inv = lax.rsqrt(total[16:24] / width + EPS)
        factor = inv * inv * inv * total[24:32] / width
        row8 = lax.broadcasted_iota(jnp.int32, (8, 128), 0)
        turned = jnp.transpose(jnp.where(row8 < 4, inv, factor))
        inv_col, factor_col = turned[:, 0:1], turned[:, 4:5]
        floats = s[u].astype(F32)
        gb[u] = (c[u].astype(F32) + inv_col * acc_g[u] - factor_col * floats).astype(BF16)
        finish(u, gb.at[u], grads_out, 1)
        zeros = jnp.zeros_like(low)
        low16 = jnp.concatenate([low * inv, zeros], axis=0).astype(BF16)
        latent16 = jnp.concatenate([latent * inv, zeros], axis=0).astype(BF16)
        ga_acc[...] += jnp.dot(low16, s[u], preferred_element_type=F32)[0:8]
        gb_acc[...] += jnp.dot(latent16, c[u], preferred_element_type=F32)[0:8]

    loads[0].wait()
    ag0(D0)
    loads[1].wait()
    build(0)
    build(1)
    rs0(D0)
    build(2)
    build(3)
    rs1(D0)
    ag1(D0)
    build(4)
    build(5)
    ag2(D0)
    rs2(D0)
    ag3(D0)
    build(6)
    rs3(D0)
    build(7)
    rev_c.wait_recv()
    rs0(U0)
    rs1(U0)
    rev_x.wait_recv()
    ag0(U0)
    for copy in loads[2:]:
        copy.wait()
    fwd_near(D0)
    rs4(D0)
    fwd_far(D0)
    ag1(U0)
    rs2(U0)
    ag2(U0)
    rs5(D0)
    rs3(U0)
    ag3(U0)
    rev_s[U0].wait_recv()
    rs4(U0)
    fwd_near(U0)
    rs5(U0)
    take_c(D0)
    rs0(D1)
    fwd_far(U0)
    rs1(D1)
    take_c(U0)
    rs0(U1)
    rs1(U1)
    take_x(U0)
    ag0(U1)
    rs2(D1)
    rs2(U1)
    ag1(U1)
    rs3(U1)
    ag2(U1)
    rs3(D1)
    ag3(U1)
    rev_s[U1].wait_recv()
    rs4(U1)
    take_x(D0)
    ag0(D1)
    fwd_near(U1)
    rs5(U1)
    fwd_far(U1)
    ag1(D1)
    ag2(D1)
    ag3(D1)
    rs4(D1)
    fwd_near(D1)
    rs5(D1)
    gar[own] = ga_acc[...] * left[rank:2 * rank, block(own)]
    mine = gar.at[own]
    shares = [
        send(mine, mine, ga_s.at[k - 1], ga_r.at[k - 1], sec, (tp + k) % n_tp)
        for k in range(1, n_tp)
    ]
    grad_b[0] = gb_acc[...].astype(BF16)
    fwd_far(D1)
    for copy in shares:
        copy.wait_recv()
    for k in range(n_tp):
        grad_a[0, :, k * cols:(k + 1) * cols] = gar[k].astype(BF16)
    for copy in outs:
        copy.wait()
    for copy in returned:
        copy.wait_recv()
    for copy in sends:
        copy.wait_send()


def body(acts_in, cots_in, stash, fresh_acts, fresh_cots, gains, weights, adapter_a, adapter_b):
    rows, cols = acts_in.shape[2], acts_in.shape[3]
    ticks = stash.shape[1]
    rank, width = adapter_a.shape[1], adapter_a.shape[2]
    n_tp = width // cols
    units = 2 * ticks
    hbm, vmem = pl.BlockSpec(memory_space=pl.ANY), pl.BlockSpec(memory_space=pltpu.VMEM)
    dma = pltpu.SemaphoreType.DMA
    tile = (rows, cols)
    out = jax.ShapeDtypeStruct((2, ticks, 1, rows, cols), BF16)
    return pl.pallas_call(
        kernel,
        name="relays",
        out_shape=(
            out,
            out,
            jax.ShapeDtypeStruct((1, rank, width), BF16),
            jax.ShapeDtypeStruct((1, rank, cols), BF16),
        ),
        in_specs=[hbm, hbm, hbm, hbm, hbm, vmem, hbm, vmem, vmem],
        out_specs=(hbm, hbm, vmem, vmem),
        scratch_shapes=[
            pltpu.VMEM((width, cols), BF16),
            pltpu.VMEM((units, n_tp) + tile, BF16),
            pltpu.VMEM((units,) + tile, BF16),
            pltpu.VMEM((units,) + tile, BF16),
            pltpu.VMEM((2,) + tile, BF16),
            pltpu.VMEM((2,) + tile, BF16),
            pltpu.VMEM((units, 7) + tile, BF16),
            pltpu.VMEM((units, 7) + tile, BF16),
            pltpu.VMEM((units,) + tile, BF16),
            pltpu.VMEM((units,) + tile, BF16),
            pltpu.VMEM((units, n_tp, 32, rows), F32),
            pltpu.VMEM((n_tp, rank, cols), F32),
            pltpu.VMEM((units,) + tile, F32),
            pltpu.VMEM((units,) + tile, F32),
            pltpu.VMEM((units, rows, 128), F32),
            pltpu.VMEM((2 * rank, width), F32),
            pltpu.VMEM((2 * rank, cols + 128), F32),
            pltpu.VMEM((rank, cols), F32),
            pltpu.VMEM((rank, cols), F32),
            dma((n_tp,)),
            dma((6,)),
            dma((4,)),
            dma((units, 7)),
            dma((units, 7)),
            dma((units, 7)),
            dma((units, 7)),
            dma((units, 7)),
            dma((units, 7)),
            dma((2, 2)),
            dma((2, 2)),
            dma((4,)),
            dma((4,)),
            dma((4,)),
            dma((4,)),
            dma((7,)),
            dma((7,)),
        ],
        compiler_params=pltpu.CompilerParams(
            collective_id=0, has_side_effects=True, vmem_limit_bytes=56 * 1024 * 1024
        ),
    )(acts_in, cots_in, stash, fresh_acts, fresh_cots, gains, weights, adapter_a, adapter_b)


def solution(mesh):
    in_specs = (
        P(None, "section", None, "tp"),
        P(None, "section", None, "tp"),
        P(None, None, "section", None, "tp"),
        P(None, None, None, "tp"),
        P(None, None, None, "tp"),
        P("section", None),
        P("section", None, "tp"),
        P("section", None, None),
        P("section", None, "tp"),
    )
    out_specs = (
        P(None, None, "section", None, "tp"),
        P(None, None, "section", None, "tp"),
        P("section", None, None),
        P("section", None, "tp"),
    )
    return jax.shard_map(body, mesh=mesh, in_specs=in_specs, out_specs=out_specs, check_vma=False)
```

time: 840 us -> 172 us (0.20)
  the two profiles are of different devices: /device:TPU:8 before, /device:TPU:32 now
where the time goes in v1:
time: 172 us; the launch traced here: 171 us
  Pallas kernels  164 us (95%)
  local copies, waits for them, and re-layouts  6.97 us (4%)
    pallas_call x1, Pallas kernels, body(): pl.pallas_call(kernel, name='relays', out_shape=(out, out, jax.ShapeDtype...  164 us
    unnamed x4, local copies, waits for them, and re-layouts  6.97 us

profile of v1, /device:TPU:32, one launch (start us, length us, event | category | flops | bytes accessed | tf_op | source)
XLA Modules:
  0.0 171.3 jit_solution(5776078188711518651)
XLA Ops:
  0.6 163.7 %relays.1 = (bf16[2,2,1,128,768]{4,3,2,1,0:T(8,128)(2,1)}, bf16[2,2,1,128,768]{4,3,2,1,0:T(8,128)(2,1)}, bf16[1,8,6144]{2,1,0:T(8,128)(2,1)}, bf16[1,8,768]{2,1,0:T(8,128)(2,1)}) custom-call(bf16[2,1,128,768]{3,2,1,0:T(8,128)(2,1)} %acts.1, bf16[2,1,128,768]{3,2,1,0:T(8,128)(2,1)} %cots.1, bf16[2,2,1,128,768]{4,3,2,1,0:T(8,128)(2,1)} %stash.1, ...), custom_call_target="tpu_custom_call" | custom-call | tf_op jit(solution)/shard_map/relays/pallas_call | solution.py:378
  164.4 2.1 %copy.17 = bf16[2,2,1,128,768]{4,3,2,1,0:T(8,128)(2,1)} copy(bf16[2,2,1,128,768]{4,3,2,1,0:T(8,128)(2,1)} %get-tuple-element.8) | data formatting | bytes 1572864
  166.4 2.1 %copy.18 = bf16[2,2,1,128,768]{4,3,2,1,0:T(8,128)(2,1)} copy(bf16[2,2,1,128,768]{4,3,2,1,0:T(8,128)(2,1)} %get-tuple-element.9) | data formatting | bytes 1572864
  168.5 1.5 copy.19
  170.0 1.3 copy.20

commit v2 on v1

--- a/solution.py
+++ b/solution.py
@@ -11,6 +11,20 @@
 BF16 = jnp.bfloat16
 
 D0, U0, D1, U1 = range(4)
+
+SCHEDULE = (
+    ("rev_x", 1), ("ag0", 0), ("build", 0), ("build", 2), ("build", 1), ("r0a", 0), ("r0b", 0), ("ag2b", 0),
+    ("ag2a", 0), ("build", 7), ("rev_c", 1), ("ag1", 0), ("ag0", 1), ("ag1", 1), ("build", 3), ("ag3", 0),
+    ("r1a", 0), ("ag2a", 1), ("build", 6), ("ag2b", 1), ("send_s", 1), ("r0a", 1), ("r0b", 1), ("build", 5),
+    ("build", 4), ("r2b", 0), ("ag3", 1), ("f0", 1), ("f2", 1), ("r1a", 1), ("f1", 1), ("r2b", 1),
+    ("r3", 0), ("f0", 0), ("f1", 0), ("r2a", 0), ("r2a", 1), ("r1b", 0), ("f3", 1), ("ox", 1),
+    ("f2", 0), ("r3", 1), ("r1b", 1), ("f3", 0), ("ag0", 3), ("r4", 0), ("r4", 1), ("ag0", 2),
+    ("r5", 0), ("ag1", 3), ("r5", 1), ("oc", 1), ("r0a", 2), ("ag2b", 3), ("ag2a", 3), ("r0a", 3),
+    ("r0b", 3), ("ag3", 3), ("r0b", 2), ("r1a", 3), ("send_s", 3), ("r2b", 3), ("f0", 3), ("r2a", 3),
+    ("f0", 2), ("r1b", 3), ("r3", 3), ("r2b", 2), ("f2", 3), ("f1", 3), ("r1a", 2), ("f3", 3),
+    ("ox", 3), ("r4", 3), ("r2a", 2), ("r1b", 2), ("r3", 2), ("r5", 3), ("oc", 3), ("ag2a", 2),
+    ("ag2b", 2), ("r4", 2), ("ag1", 2), ("ag3", 2), ("r5", 2), ("f1", 2), ("f2", 2), ("f3", 2),
+)
 
 
 def contract_last(left, right):
@@ -80,12 +94,17 @@
         pl.semaphore_signal(barrier, inc=1, device_id=peer, device_id_type=MESH)
     pl.semaphore_wait(barrier, len(peers))
 
-    rev_c = send(cots.at[1, 0], c.at[U0], ri_s.at[0], ri_r.at[0], mirror, tp)
-    rev_x = send(acts.at[1, 0], x.at[U0, own], ri_s.at[1], ri_r.at[1], mirror, tp)
-    rev_s = {
-        U0: send(stash.at[1, 0, 0], s.at[U0], ri_s.at[2], ri_r.at[2], mirror, tp),
-        U1: send(stash.at[1, 1, 0], s.at[U1], ri_s.at[3], ri_r.at[3], mirror, tp),
-    }
+    turned_in = {}
+
+    def rev_c(u):
+        turned_in["c"] = send(cots.at[1, 0], c.at[u], ri_s.at[0], ri_r.at[0], mirror, tp)
+
+    def rev_x(u):
+        turned_in["x"] = send(acts.at[1, 0], x.at[u, own], ri_s.at[1], ri_r.at[1], mirror, tp)
+
+    def rev_s(u):
+        tick = u // 2
+        turned_in[u] = send(stash.at[1, tick, 0], s.at[u], ri_s.at[2 + tick], ri_r.at[2 + tick], mirror, tp)
 
     left[0:rank] = lower[0].astype(F32)
     left[rank:2 * rank] = jnp.broadcast_to(gain[...].astype(F32), (rank, width))
@@ -112,33 +131,43 @@
 
         lax.fori_loop(0, cols // 128, step, 0)
 
-    gathered = {}
+    gathered, here = {}, set()
+
+    def arrive(u, i):
+        if (u, i) not in here:
+            here.add((u, i))
+            gathered[u][i].wait_recv()
 
     def ag0(u):
         mine = x.at[u, own]
-        gathered[u] = [
-            send(mine, mine, ag_s.at[u, 0], ag_r.at[u, 0], sec, across),
-            send(mine, mine, ag_s.at[u, 1], ag_r.at[u, 1], sec, pp),
-            send(mine, mine, ag_s.at[u, 2], ag_r.at[u, 2], sec, mm),
-        ]
+        gathered[u] = {
+            i: send(mine, mine, ag_s.at[u, i], ag_r.at[u, i], sec, to_tp)
+            for i, to_tp in enumerate((across, pp, mm))
+        }
 
     def ag1(u):
-        gathered[u][0].wait_recv()
+        arrive(u, 0)
         part = x.at[u, across]
-        gathered[u] += [
-            send(part, part, ag_s.at[u, 3], ag_r.at[u, 3], sec, pp),
-            send(part, part, ag_s.at[u, 4], ag_r.at[u, 4], sec, mm),
-        ]
-
-    def ag2(u):
-        gathered[u][1].wait_recv()
-        part = x.at[u, mm]
-        gathered[u].append(send(part, part, ag_s.at[u, 5], ag_r.at[u, 5], sec, pp))
+        for i, to_tp in ((3, pp), (4, mm)):
+            gathered[u][i] = send(part, part, ag_s.at[u, i], ag_r.at[u, i], sec, to_tp)
+
+    def ag2(u, k, wait, which, to_tp):
+        half = x.shape[2] // 2
+        arrive(u, wait)
+        piece = x.at[u, which, pl.ds(k * half, half)]
+        gathered[u][5 + k] = send(piece, piece, ag_s.at[u, 5 + k], ag_r.at[u, 5 + k], sec, to_tp)
+
+    def ag2a(u):
+        ag2(u, 0, 1, mm, pp)
+
+    def ag2b(u):
+        ag2(u, 1, 2, pp, mm)
 
     def ag3(u):
-        gathered[u][4].wait_recv()
-        part = x.at[u, po]
-        gathered[u].append(send(part, part, ag_s.at[u, 6], ag_r.at[u, 6], sec, mm))
+        arrive(u, 5)
+        arrive(u, 6)
+        far = x.at[u, tt]
+        gathered[u][7] = send(far, far, ag_s.at[u, 7], ag_r.at[u, 7], sec, across)
 
     def fwd(u, which, first=False):
         rows = x[u, which]
@@ -155,20 +184,24 @@
             sq[u] += total
             acc[u] += product
 
-    def fwd_near(u):
+    def f0(u):
         fwd(u, own, True)
-        fwd(u, across)
-        fwd(u, mm)
-        gathered[u][2].wait_recv()
-        fwd(u, pp)
-        gathered[u][3].wait_recv()
-        fwd(u, mo)
-        fwd(u, po)
-
-    def fwd_far(u):
-        gathered[u][5].wait_recv()
+        for i, which in ((1, mm), (2, pp), (0, across)):
+            arrive(u, i)
+            fwd(u, which)
+
+    def f1(u):
+        for i, which in ((3, mo), (4, po)):
+            arrive(u, i)
+            fwd(u, which)
+
+    def f2(u):
+        arrive(u, 5)
+        arrive(u, 6)
         fwd(u, tt)
-        gathered[u][6].wait_recv()
+
+    def f3(u):
+        arrive(u, 7)
         fwd(u, to)
         inv = lax.rsqrt(jnp.sum(sq[u], axis=1, keepdims=True) / width + EPS)
         yb[u] = (x[u, own].astype(F32) + inv * acc[u]).astype(BF16)
@@ -187,12 +220,28 @@
             copy = pltpu.make_async_copy(result, out.at[0, tick, 0], out_sem.at[tick * 2 + which])
             copy.start()
             outs.append(copy)
-        else:
-            k = tick * 2 + which
-            returned.append(send(result, out.at[1, tick, 0], ro_s.at[k], ro_r.at[k], mirror, tp))
+
+    def turn_out(u, result, out, which):
+        tick = u // 2
+        k = tick * 2 + which
+        returned.append(send(result, out.at[1, tick, 0], ro_s.at[k], ro_r.at[k], mirror, tp))
+
+    def ox(u):
+        turn_out(u, yb.at[u], acts_out, 0)
+
+    def oc(u):
+        turn_out(u, gb.at[u], grads_out, 1)
+
+    taken = set()
+
+    def fresh(i):
+        if i not in taken:
+            taken.add(i)
+            loads[i].wait()
 
     def take_x(u):
         shifted[u, 0].wait_recv()
+        fresh(4)
 
         @pl.when(sec == 0)
         def _():
@@ -200,6 +249,7 @@
 
     def take_c(u):
         shifted[u, 1].wait_recv()
+        fresh(5)
 
         @pl.when(sec == n_sec - 1)
         def _():
@@ -220,22 +270,35 @@
         reduced[u][i].wait_recv()
         return pr[u, i].astype(F32)
 
-    def rs0(u):
+    def r0a(u):
         rs_send(u, 0, part(u, tt), pp)
+
+    def r0b(u):
         rs_send(u, 1, part(u, to), mm)
 
-    def rs1(u):
+    def r1a(u):
         rs_send(u, 2, part(u, po), pp)
+
+    def r1b(u):
         rs_send(u, 3, part(u, mm), mm)
 
-    def rs2(u):
+    def r2a(u):
         rs_send(u, 4, part(u, pp) + got(u, 0), pp)
+
+    def r2b(u):
         rs_send(u, 5, part(u, mo) + got(u, 1), mm)
 
-    def rs3(u):
+    def r3(u):
         rs_send(u, 6, part(u, across) + got(u, 5) + got(u, 2), across)
 
     summed = {}
+    row8 = lax.broadcasted_iota(jnp.int32, (8, 128), 0)
+
+    def three_terms(value):
+        first = value.astype(BF16).astype(F32)
+        second = (value - first).astype(BF16).astype(F32)
+        third = value - first - second
+        return jnp.where(row8 == 0, first, jnp.where(row8 == 1, second, jnp.where(row8 == 2, third, 0.0)))
 
     def split_sum(value):
         ones = jnp.ones((16, cols), BF16)
@@ -243,30 +306,31 @@
         low = (value - high.astype(F32)).astype(BF16)
         return (contract_last(ones, high) + contract_last(ones, low))[0:8]
 
-    def rs4(u):
-        total = part(u, own) + got(u, 4) + got(u, 3) + got(u, 6)
-        acc_g[u] = total
+    def r4(u):
         floats = s[u].astype(F32)
         at = block(own)
         pair = jnp.concatenate([left[0:rank, at] * left[rank:2 * rank, at], right[0:rank, 0:cols]], axis=0).astype(BF16)
-        sm[u, own, 0:8] = contract_last(pair, c[u])[8:16]
-        sm[u, own, 8:16] = contract_last(pair, s[u])[0:8]
-        sm[u, own, 16:24] = split_sum(floats * floats)
-        sm[u, own, 24:32] = split_sum(floats * total)
+        sm[u, own, 0:16] = jnp.concatenate(
+            [contract_last(pair, c[u])[8:16], contract_last(pair, s[u])[0:8]], axis=0
+        ).astype(BF16)
+        squares = three_terms(split_sum(floats * floats))
+        total = part(u, own) + got(u, 4) + got(u, 3) + got(u, 6)
+        acc_g[u] = total
+        crossed = three_terms(split_sum(s[u].astype(F32) * total))
+        sm[u, own, 16:32] = jnp.concatenate([squares, crossed], axis=0).astype(BF16)
         mine = sm.at[u, own]
         summed[u] = [
             send(mine, mine, sm_s.at[u, k - 1], sm_r.at[u, k - 1], sec, (tp + k) % n_tp)
             for k in range(1, n_tp)
         ]
 
-    def rs5(u):
+    def r5(u):
         for copy in summed[u]:
             copy.wait_recv()
-        total = jnp.sum(sm[u], axis=0)
+        total = jnp.sum(sm[u].astype(F32), axis=0)
         low, latent = total[0:8], total[8:16]
-        inv = lax.rsqrt(total[16:24] / width + EPS)
-        factor = inv * inv * inv * total[24:32] / width
-        row8 = lax.broadcasted_iota(jnp.int32, (8, 128), 0)
+        inv = lax.rsqrt(jnp.sum(total[16:24], axis=0, keepdims=True) / width + EPS)
+        factor = inv * inv * inv * jnp.sum(total[24:32], axis=0, keepdims=True) / width
         turned = jnp.transpose(jnp.where(row8 < 4, inv, factor))
         inv_col, factor_col = turned[:, 0:1], turned[:, 4:5]
         floats = s[u].astype(F32)
@@ -278,91 +342,77 @@
         ga_acc[...] += jnp.dot(low16, s[u], preferred_element_type=F32)[0:8]
         gb_acc[...] += jnp.dot(latent16, c[u], preferred_element_type=F32)[0:8]
 
-    loads[0].wait()
-    ag0(D0)
-    loads[1].wait()
-    build(0)
-    build(1)
-    rs0(D0)
-    build(2)
-    build(3)
-    rs1(D0)
-    ag1(D0)
-    build(4)
-    build(5)
-    ag2(D0)
-    rs2(D0)
-    ag3(D0)
-    build(6)
-    rs3(D0)
-    build(7)
-    rev_c.wait_recv()
-    rs0(U0)
-    rs1(U0)
-    rev_x.wait_recv()
-    ag0(U0)
-    for copy in loads[2:]:
-        copy.wait()
-    fwd_near(D0)
-    rs4(D0)
-    fwd_far(D0)
-    ag1(U0)
-    rs2(U0)
-    ag2(U0)
-    rs5(D0)
-    rs3(U0)
-    ag3(U0)
-    rev_s[U0].wait_recv()
-    rs4(U0)
-    fwd_near(U0)
-    rs5(U0)
-    take_c(D0)
-    rs0(D1)
-    fwd_far(U0)
-    rs1(D1)
-    take_c(U0)
-    rs0(U1)
-    rs1(U1)
-    take_x(U0)
-    ag0(U1)
-    rs2(D1)
-    rs2(U1)
-    ag1(U1)
-    rs3(U1)
-    ag2(U1)
-    rs3(D1)
-    ag3(U1)
-    rev_s[U1].wait_recv()
-    rs4(U1)
-    take_x(D0)
-    ag0(D1)
-    fwd_near(U1)
-    rs5(U1)
-    fwd_far(U1)
-    ag1(D1)
-    ag2(D1)
-    ag3(D1)
-    rs4(D1)
-    fwd_near(D1)
-    rs5(D1)
-    gar[own] = ga_acc[...] * left[rank:2 * rank, block(own)]
-    mine = gar.at[own]
-    shares = [
-        send(mine, mine, ga_s.at[k - 1], ga_r.at[k - 1], sec, (tp + k) % n_tp)
-        for k in range(1, n_tp)
-    ]
-    grad_b[0] = gb_acc[...].astype(BF16)
-    fwd_far(D1)
+    def begin_c(u):
+        if u == D0:
+            loads[1].wait()
+        elif u == U0:
+            turned_in["c"].wait_recv()
+        else:
+            take_c(u - 2)
+        r0a(u)
+
+    def begin_x(u):
+        if u == D0:
+            loads[0].wait()
+        elif u == U0:
+            turned_in["x"].wait_recv()
+        else:
+            take_x(u - 2)
+        ag0(u)
+
+    def begin_s(u):
+        if u in (U0, U1):
+            turned_in[u].wait_recv()
+        else:
+            loads[2 + u // 2].wait()
+        r4(u)
+
+    shares = []
+
+    def share_a():
+        gar[own] = ga_acc[...] * left[rank:2 * rank, block(own)]
+        mine = gar.at[own]
+        for k in range(1, n_tp):
+            shares.append(send(mine, mine, ga_s.at[k - 1], ga_r.at[k - 1], sec, (tp + k) % n_tp))
+        grad_b[0] = gb_acc[...]
+
+    steps = {
+        "build": build, "rev_c": rev_c, "rev_x": rev_x, "send_s": rev_s,
+        "ag0": begin_x, "ag1": ag1, "ag2a": ag2a, "ag2b": ag2b, "ag3": ag3,
+        "f0": f0, "f1": f1, "f2": f2, "f3": f3,
+        "r0a": begin_c, "r0b": r0b, "r1a": r1a, "r1b": r1b, "r2a": r2a, "r2b": r2b, "r3": r3,
+        "r4": begin_s, "r5": r5, "ox": ox, "oc": oc,
+    }
+    last = [which for which in SCHEDULE if which[0] == "r5"][-1]
+    for step, u in SCHEDULE:
+        steps[step](u)
+        if (step, u) == last:
+            share_a()
     for copy in shares:
         copy.wait_recv()
     for k in range(n_tp):
-        grad_a[0, :, k * cols:(k + 1) * cols] = gar[k].astype(BF16)
+        grad_a[0, :, k * cols:(k + 1) * cols] = gar[k]
     for copy in outs:
         copy.wait()
     for copy in returned:
         copy.wait_recv()
     for copy in sends:
         copy.wait_send()
+
+
+def settle(acts, grads, sum_a, sum_b, acts_out, grads_out, grad_a, grad_b, held, sem_in, sem_out):
+    pairs = [(src, dst, r, k) for r in range(2) for k in range(acts.shape[1]) for src, dst in ((acts, acts_out), (grads, grads_out))]
+    takes = [pltpu.make_async_copy(src.at[r, k, 0], held.at[i], sem_in.at[i]) for i, (src, dst, r, k) in enumerate(pairs)]
+    gives = [pltpu.make_async_copy(held.at[i], dst.at[r, k, 0], sem_out.at[i]) for i, (src, dst, r, k) in enumerate(pairs)]
+    for take in takes:
+        take.start()
+    grad_a[...] = sum_a[...].astype(BF16)
+    grad_b[...] = sum_b[...].astype(BF16)
+    for take, give in zip(takes, gives):
+        take.wait()
+        give.start()
+    for give in gives:
+        give.wait()
 
 
 def body(acts_in, cots_in, stash, fresh_acts, fresh_cots, gains, weights, adapter_a, adapter_b):
@@ -375,14 +425,14 @@
     dma = pltpu.SemaphoreType.DMA
     tile = (rows, cols)
     out = jax.ShapeDtypeStruct((2, ticks, 1, rows, cols), BF16)
-    return pl.pallas_call(
+    results = pl.pallas_call(
         kernel,
         name="relays",
         out_shape=(
             out,
             out,
-            jax.ShapeDtypeStruct((1, rank, width), BF16),
-            jax.ShapeDtypeStruct((1, rank, cols), BF16),
+            jax.ShapeDtypeStruct((1, rank, width), F32),
+            jax.ShapeDtypeStruct((1, rank, cols), F32),
         ),
         in_specs=[hbm, hbm, hbm, hbm, hbm, vmem, hbm, vmem, vmem],
         out_specs=(hbm, hbm, vmem, vmem),
@@ -397,7 +447,7 @@
             pltpu.VMEM((units, 7) + tile, BF16),
             pltpu.VMEM((units,) + tile, BF16),
             pltpu.VMEM((units,) + tile, BF16),
-            pltpu.VMEM((units, n_tp, 32, rows), F32),
+            pltpu.VMEM((units, n_tp, 32, rows), BF16),
             pltpu.VMEM((n_tp, rank, cols), F32),
             pltpu.VMEM((units,) + tile, F32),
             pltpu.VMEM((units,) + tile, F32),
@@ -409,8 +459,8 @@
             dma((n_tp,)),
             dma((6,)),
             dma((4,)),
-            dma((units, 7)),
-            dma((units, 7)),
+            dma((units, 8)),
+            dma((units, 8)),
             dma((units, 7)),
             dma((units, 7)),
             dma((units, 7)),
@@ -428,6 +478,19 @@
             collective_id=0, has_side_effects=True, vmem_limit_bytes=56 * 1024 * 1024
         ),
     )(acts_in, cots_in, stash, fresh_acts, fresh_cots, gains, weights, adapter_a, adapter_b)
+    return pl.pallas_call(
+        settle,
+        name="settle",
+        out_shape=(
+            out,
+            out,
+            jax.ShapeDtypeStruct((1, rank, width), BF16),
+            jax.ShapeDtypeStruct((1, rank, cols), BF16),
+        ),
+        in_specs=[hbm, hbm, vmem, vmem],
+        out_specs=(hbm, hbm, vmem, vmem),
+        scratch_shapes=[pltpu.VMEM((4 * ticks,) + tile, BF16), dma((4 * ticks,)), dma((4 * ticks,))],
+    )(*results)
 
 
 def solution(mesh):

time: 172 us -> 139 us (0.81)
  the two profiles are of different devices: /device:TPU:32 before, /device:TPU:8 now
where the time goes in v2:
time: 139 us
  Pallas kernels  138 us (99%)
    pallas_call x1, Pallas kernels, body(): pl.pallas_call(kernel, name='relays', out_shape=(out, out, jax.ShapeDtype...  134 us
    pallas_call x1, Pallas kernels, body(): pl.pallas_call(settle, name='settle', out_shape=(out, out, jax.ShapeDtype...  3.87 us

profile of v2, /device:TPU:8, one launch (start us, length us, event | category | flops | bytes accessed | tf_op | source)
XLA Modules:
  0.0 139.1 jit_solution(5731485243185896725)
XLA Ops:
  0.6 134.4 %relays.1 = (bf16[2,2,1,128,768]{4,3,2,1,0:T(8,128)(2,1)}, bf16[2,2,1,128,768]{4,3,2,1,0:T(8,128)(2,1)}, f32[1,8,6144]{2,1,0:T(8,128)}, f32[1,8,768]{2,1,0:T(8,128)}) custom-call(bf16[2,1,128,768]{3,2,1,0:T(8,128)(2,1)} %acts.1, bf16[2,1,128,768]{3,2,1,0:T(8,128)(2,1)} %cots.1, bf16[2,2,1,128,768]{4,3,2,1,0:T(8,128)(2,1)} %stash.1, ...), custom_call_target="tpu_custom_call" | custom-call | tf_op jit(solution)/shard_map/relays/pallas_call | solution.py:428
  135.0 3.9 %settle.1 = (bf16[2,2,1,128,768]{4,3,2,1,0:T(8,128)(2,1)}, bf16[2,2,1,128,768]{4,3,2,1,0:T(8,128)(2,1)}, bf16[1,8,6144]{2,1,0:T(8,128)(2,1)}, bf16[1,8,768]{2,1,0:T(8,128)(2,1)}) custom-call(bf16[2,2,1,128,768]{4,3,2,1,0:T(8,128)(2,1)} %get-tuple-element.8.acts, bf16[2,2,1,128,768]{4,3,2,1,0:T(8,128)(2,1)} %get-tuple-element.9.grads, ...), custom_call_target="tpu_custom_call" | custom-call | tf_op jit(solution)/shard_map/settle/pallas_call | solution.py:481

commit v3 on v2

--- a/solution.py
+++ b/solution.py
@@ -13,17 +13,17 @@
 D0, U0, D1, U1 = range(4)
 
 SCHEDULE = (
-    ("rev_x", 1), ("ag0", 0), ("build", 0), ("build", 2), ("build", 1), ("r0a", 0), ("r0b", 0), ("ag2b", 0),
-    ("ag2a", 0), ("build", 7), ("rev_c", 1), ("ag1", 0), ("ag0", 1), ("ag1", 1), ("build", 3), ("ag3", 0),
-    ("r1a", 0), ("ag2a", 1), ("build", 6), ("ag2b", 1), ("send_s", 1), ("r0a", 1), ("r0b", 1), ("build", 5),
-    ("build", 4), ("r2b", 0), ("ag3", 1), ("f0", 1), ("f2", 1), ("r1a", 1), ("f1", 1), ("r2b", 1),
-    ("r3", 0), ("f0", 0), ("f1", 0), ("r2a", 0), ("r2a", 1), ("r1b", 0), ("f3", 1), ("ox", 1),
-    ("f2", 0), ("r3", 1), ("r1b", 1), ("f3", 0), ("ag0", 3), ("r4", 0), ("r4", 1), ("ag0", 2),
-    ("r5", 0), ("ag1", 3), ("r5", 1), ("oc", 1), ("r0a", 2), ("ag2b", 3), ("ag2a", 3), ("r0a", 3),
-    ("r0b", 3), ("ag3", 3), ("r0b", 2), ("r1a", 3), ("send_s", 3), ("r2b", 3), ("f0", 3), ("r2a", 3),
-    ("f0", 2), ("r1b", 3), ("r3", 3), ("r2b", 2), ("f2", 3), ("f1", 3), ("r1a", 2), ("f3", 3),
-    ("ox", 3), ("r4", 3), ("r2a", 2), ("r1b", 2), ("r3", 2), ("r5", 3), ("oc", 3), ("ag2a", 2),
-    ("ag2b", 2), ("r4", 2), ("ag1", 2), ("ag3", 2), ("r5", 2), ("f1", 2), ("f2", 2), ("f3", 2),
+    ("ag0", 0), ("rev_x", 1), ("build", 0), ("r0a", 0), ("build", 1), ("ag2b", 0), ("r0b", 0), ("build", 3),
+    ("ag2a", 0), ("build", 2), ("ag0", 1), ("rev_c", 1), ("build", 5), ("r1a", 0), ("build", 4), ("r2b", 0),
+    ("build", 7), ("r1b", 0), ("r2a", 0), ("build", 6), ("r0a", 1), ("r3", 0), ("r0b", 1), ("f0", 0),
+    ("r4", 0), ("ag2b", 1), ("send_s", 1), ("ag3", 0), ("ag2a", 1), ("r1a", 1), ("r2b", 1), ("ag1", 1),
+    ("f2", 0), ("f0", 1), ("r5", 0), ("ag3", 1), ("f2", 1), ("r2a", 1), ("r1b", 1), ("r3", 1),
+    ("ag1", 0), ("r0a", 2), ("f1", 1), ("r0b", 2), ("r4", 1), ("f3", 1), ("r1b", 2), ("send_s", 3),
+    ("r1a", 2), ("r5", 1), ("ag0", 3), ("ox", 1), ("r2b", 2), ("r0a", 3), ("ag2a", 3), ("oc", 1),
+    ("r0b", 3), ("f1", 0), ("r1a", 3), ("f0", 3), ("ag2b", 3), ("r3", 2), ("r2b", 3), ("ag3", 3),
+    ("ag1", 3), ("f3", 0), ("f2", 3), ("r2a", 3), ("r3", 3), ("r1b", 3), ("r2a", 2), ("f1", 3),
+    ("f3", 3), ("ox", 3), ("r4", 3), ("ag0", 2), ("r4", 2), ("r5", 3), ("oc", 3), ("ag2b", 2),
+    ("ag2a", 2), ("r5", 2), ("ag1", 2), ("ag3", 2), ("f0", 2), ("f2", 2), ("f1", 2), ("f3", 2),
 )
 
 

time: 139 us -> 137 us (0.986)
  Pallas kernels: 138 us -> 136 us
    pallas_call x1, Pallas kernels: 134 us -> 133 us  [body(): pl.pallas_call(kernel, name='relays', out_shape=(out, out, jax.ShapeDtype...]
where the time goes in v3:
time: 137 us
  Pallas kernels  136 us (99%)
    pallas_call x1, Pallas kernels, body(): pl.pallas_call(kernel, name='relays', out_shape=(out, out, jax.ShapeDtype...  133 us
    pallas_call x1, Pallas kernels, body(): pl.pallas_call(settle, name='settle', out_shape=(out, out, jax.ShapeDtype...  3.87 us

profile of v3, /device:TPU:8, one launch (start us, length us, event | category | flops | bytes accessed | tf_op | source)
XLA Modules:
  0.0 137.3 jit_solution(12066401425636585200)
XLA Ops:
  0.6 132.6 %relays.1 = (bf16[2,2,1,128,768]{4,3,2,1,0:T(8,128)(2,1)}, bf16[2,2,1,128,768]{4,3,2,1,0:T(8,128)(2,1)}, f32[1,8,6144]{2,1,0:T(8,128)}, f32[1,8,768]{2,1,0:T(8,128)}) custom-call(bf16[2,1,128,768]{3,2,1,0:T(8,128)(2,1)} %acts.1, bf16[2,1,128,768]{3,2,1,0:T(8,128)(2,1)} %cots.1, bf16[2,2,1,128,768]{4,3,2,1,0:T(8,128)(2,1)} %stash.1, ...), custom_call_target="tpu_custom_call" | custom-call | tf_op jit(solution)/shard_map/relays/pallas_call | solution.py:428
  133.2 3.9 %settle.1 = (bf16[2,2,1,128,768]{4,3,2,1,0:T(8,128)(2,1)}, bf16[2,2,1,128,768]{4,3,2,1,0:T(8,128)(2,1)}, bf16[1,8,6144]{2,1,0:T(8,128)(2,1)}, bf16[1,8,768]{2,1,0:T(8,128)(2,1)}) custom-call(bf16[2,2,1,128,768]{4,3,2,1,0:T(8,128)(2,1)} %get-tuple-element.8.acts, bf16[2,2,1,128,768]{4,3,2,1,0:T(8,128)(2,1)} %get-tuple-element.9.grads, ...), custom_call_target="tpu_custom_call" | custom-call | tf_op jit(solution)/shard_map/settle/pallas_call | solution.py:481

commit v4 on v3

--- a/solution.py
+++ b/solution.py
@@ -211,10 +211,20 @@
 
     def finish(u, result, out, which):
         if u < 2:
-            if which == 0:
-                shifted[u, 0] = send(result, x.at[u + 2, own], sh_s.at[u, 0], sh_r.at[u, 0], ahead, tp)
-            else:
-                shifted[u, 1] = send(result, c.at[u + 2], sh_s.at[u, 1], sh_r.at[u, 1], behind, tp)
+            target = c.at[u + 2] if which else x.at[u + 2, own]
+
+            def shift():
+                return pltpu.make_async_remote_copy(
+                    src_ref=result, dst_ref=target, send_sem=sh_s.at[u, which], recv_sem=sh_r.at[u, which],
+                    device_id=(behind if which else ahead, tp), device_id_type=MESH,
+                )
+
+            shifted[u, which] = shift
+
+            @pl.when(sec != (0 if which else n_sec - 1))
+            def _():
+                shift().start()
+
         tick, relay = u // 2, u % 2
         if relay == 0:
             copy = pltpu.make_async_copy(result, out.at[0, tick, 0], out_sem.at[tick * 2 + which])
@@ -240,16 +250,22 @@
             loads[i].wait()
 
     def take_x(u):
-        shifted[u, 0].wait_recv()
         fresh(4)
+
+        @pl.when(sec != 0)
+        def _():
+            shifted[u, 0]().wait_recv()
 
         @pl.when(sec == 0)
         def _():
             x[u + 2, own] = fa[u]
 
     def take_c(u):
-        shifted[u, 1].wait_recv()
         fresh(5)
+
+        @pl.when(sec != n_sec - 1)
+        def _():
+            shifted[u, 1]().wait_recv()
 
         @pl.when(sec == n_sec - 1)
         def _():
@@ -398,6 +414,12 @@
         copy.wait_recv()
     for copy in sends:
         copy.wait_send()
+    for which, final in ((0, n_sec - 1), (1, 0)):
+
+        @pl.when(sec != final)
+        def _():
+            for u in (D0, U0):
+                shifted[u, which]().wait_send()
 
 
 def settle(acts, grads, sum_a, sum_b, acts_out, grads_out, grad_a, grad_b, held, sem_in, sem_out):

time: 137 us -> 138 us (level)
  Pallas kernels: 136 us -> 138 us
where the time goes in v4:
time: 138 us
  Pallas kernels  138 us (100%)
    pallas_call x1, Pallas kernels, body(): pl.pallas_call(kernel, name='relays', out_shape=(out, out, jax.ShapeDtype...  134 us
    pallas_call x1, Pallas kernels, body(): pl.pallas_call(settle, name='settle', out_shape=(out, out, jax.ShapeDtype...  3.87 us

profile of v4, /device:TPU:8, one launch (start us, length us, event | category | flops | bytes accessed | tf_op | source)
XLA Modules:
  0.0 138.3 jit_solution(4496567670185559102)
XLA Ops:
  0.6 133.6 %relays.1 = (bf16[2,2,1,128,768]{4,3,2,1,0:T(8,128)(2,1)}, bf16[2,2,1,128,768]{4,3,2,1,0:T(8,128)(2,1)}, f32[1,8,6144]{2,1,0:T(8,128)}, f32[1,8,768]{2,1,0:T(8,128)}) custom-call(bf16[2,1,128,768]{3,2,1,0:T(8,128)(2,1)} %acts.1, bf16[2,1,128,768]{3,2,1,0:T(8,128)(2,1)} %cots.1, bf16[2,2,1,128,768]{4,3,2,1,0:T(8,128)(2,1)} %stash.1, ...), custom_call_target="tpu_custom_call" | custom-call | tf_op jit(solution)/shard_map/relays/pallas_call | solution.py:450
  134.3 3.9 %settle.1 = (bf16[2,2,1,128,768]{4,3,2,1,0:T(8,128)(2,1)}, bf16[2,2,1,128,768]{4,3,2,1,0:T(8,128)(2,1)}, bf16[1,8,6144]{2,1,0:T(8,128)(2,1)}, bf16[1,8,768]{2,1,0:T(8,128)(2,1)}) custom-call(bf16[2,2,1,128,768]{4,3,2,1,0:T(8,128)(2,1)} %get-tuple-element.8.acts, bf16[2,2,1,128,768]{4,3,2,1,0:T(8,128)(2,1)} %get-tuple-element.9.grads, ...), custom_call_target="tpu_custom_call" | custom-call | tf_op jit(solution)/shard_map/settle/pallas_call | solution.py:503
